TPU v7x, 128 devices: a whole 4x4x4 slice. The times are simulated.
128 devices in a mesh: img: 32 (over y, x, core), ch: 4 (over z).
Axes of the slice: x: 4, y: 4, z: 4, core: 2. Of those that a mesh axis runs over, the one named last changes fastest.
Arguments:
- canvas: bfloat16 [1024, 32, 1536], P('img', None, 'ch'), may hold values from -6 to 6
- screen_size: int32 [32, 2], P('img'), may hold values from 8 to 32, as said below
- tile_counts: int32 [32], replicated, may hold values from 1 to 32, 512 in all
- tile_offsets: int32 [1024, 2], P('img'), may hold values from 0 to 28, as said below
- cotangent: bfloat16 [1024, 4, 4, 1536], P('img', None, None, 'ch'), may hold values from -6 to 6
- dw_kernel: bfloat16 [49, 1536], P(None, 'ch'), may hold values from -0.875 to 0.875
- dw_bias: float32 [1536], P('ch'), may hold values from -3 to 3
- ln_gain: float32 [1536], replicated, may hold values from 0.5 to 1.5
- ln_bias: float32 [1536], replicated, may hold values from -0.5 to 0.5
- w_in: bfloat16 [1536, 6144], P(None, 'ch'), may hold values from -0.15625 to 0.15625
- b_in: float32 [6144], P('ch'), may hold values from -1 to 1
- w_out: bfloat16 [6144, 1536], P('ch'), may hold values from -0.078125 to 0.078125
- layer_scale: float32 [1536], replicated, may hold values from 0.25 to 2
Outputs:
- grad_canvas: float32 [1024, 32, 1536], P('img', None, 'ch')
Inputs may be any that keep to these rules, and one draw needn't show every extreme that they name: `tile_counts`: the counts sum to 512 and the largest is exactly 32. `screen_size`: some screenshot is 32 by 32 cells. `tile_offsets`: every slot's interior lies inside its screenshot.
All inputs are finite; a program needn't handle non-finite values.
Results may differ from a plain program's by a relative error of at most 0.0031.
Values may be sent and summed in bfloat16 or wider, within the bound.
No kernel may reach another device: no remote copies, remote signals or barrier semaphores. Data moves between devices by JAX's collectives and lax.ppermute only.
A program may use at most 128 MiB of HBM per device.

v0:
```python
import jax
import jax.numpy as jnp
from jax import lax
from jax.sharding import PartitionSpec as P

TS = 4
slope_coef = 0.7978845608
cubic_coef = 0.044715
norm_eps = 1e-06


def gelu_slope(pre_act):
    inner_arg = slope_coef * (pre_act + cubic_coef * pre_act * pre_act * pre_act)
    tangent = jnp.tanh(inner_arg)
    return 0.5 * (1.0 + tangent) + 0.5 * pre_act * (1.0 - tangent * tangent) * slope_coef * (
        1.0 + 3.0 * cubic_coef * pre_act * pre_act
    )


def depthwise(patches, kernel, bias):
    result = jnp.zeros((patches.shape[0], TS, TS, patches.shape[3]), jnp.float32) + bias
    for offset_r in range(7):
        for offset_c in range(7):
            result = result + patches[
                :, offset_r : offset_r + TS, offset_c : offset_c + TS, :
            ].astype(jnp.float32) * kernel[offset_r * 7 + offset_c].astype(jnp.float32)
    return result


def depthwise_back(upstream, kernel):
    result = jnp.zeros((upstream.shape[0], TS + 6, TS + 6, upstream.shape[3]), jnp.float32)
    for offset_r in range(7):
        for offset_c in range(7):
            result = result.at[:, offset_r : offset_r + TS, offset_c : offset_c + TS, :].add(
                upstream * kernel[offset_r * 7 + offset_c].astype(jnp.float32)
            )
    return result


def shards(
    canvas,
    screen_size,
    tile_counts,
    tile_offsets,
    cotangent,
    dw_kernel,
    dw_bias,
    ln_gain,
    ln_bias,
    w_in,
    b_in,
    w_out,
    layer_scale,
):
    owners = lax.axis_size("img")
    my_owner = lax.axis_index("img")
    my_part = lax.axis_index("ch")
    side = canvas.shape[0]
    share = canvas.shape[2]
    most = tile_offsets.shape[0]
    width = ln_gain.shape[0]
    framed_side = TS + 6
    per_pair = -(-most // owners)
    buffer_len = owners * per_pair
    lines = jnp.arange(side, dtype=jnp.int32)
    inside = (lines[:, None] < screen_size[0, 0]) & (lines[None, :] < screen_size[0, 1])
    masked = jnp.where(inside[:, :, None], canvas, jnp.zeros_like(canvas))
    framed = jnp.pad(masked, ((3, 3), (3, 3), (0, 0)))
    patches = jax.vmap(
        lambda corner: lax.dynamic_slice(
            framed, (corner[0], corner[1], jnp.int32(0)), (framed_side, framed_side, share)
        )
    )(tile_offsets)
    slots = jnp.arange(most, dtype=jnp.int32)
    owner_ids = jnp.arange(owners, dtype=jnp.int32)
    my_count = jnp.sum(jnp.where(owner_ids == my_owner, tile_counts, 0))
    classes = min(most, owners)
    slot_class = slots % classes
    base = slot_class * owners // classes
    spread_off = jnp.where(
        slot_class == 1, 1, jnp.where(slot_class == classes - 1, owners - 1, base)
    )
    target = (my_owner + spread_off) % owners
    source = (my_owner - spread_off) % owners
    pick = source * per_pair + slots // classes
    position = target * per_pair + slots // classes
    send_cot = jnp.zeros((buffer_len, TS, TS, share), jnp.bfloat16).at[position].set(cotangent)
    send_tiles = (
        jnp.zeros((buffer_len, framed_side, framed_side, share), jnp.bfloat16)
        .at[position]
        .set(patches)
    )
    got_tiles, got_cot = (
        lax.all_to_all(send_tiles, "img", split_axis=0, concat_axis=0, tiled=True),
        lax.all_to_all(send_cot, "img", split_axis=0, concat_axis=0, tiled=True),
    )
    mixed = depthwise(got_tiles[pick], dw_kernel, dw_bias).astype(jnp.bfloat16)
    cot_mine = got_cot[pick]
    gathered, cot_full = (
        lax.all_gather(mixed, "ch", axis=3, tiled=True),
        lax.all_gather(cot_mine, "ch", axis=3, tiled=True),
    )
    values = gathered.astype(jnp.float32)
    center = jnp.mean(values, axis=3, keepdims=True)
    spread = jnp.mean(jnp.square(values - center), axis=3, keepdims=True)
    inv_std = lax.rsqrt(spread + norm_eps)
    normed = (values - center) * inv_std
    scaled = (normed * ln_gain + ln_bias).astype(jnp.bfloat16)
    row_count = most * TS * TS
    pre_act = (
        jnp.dot(scaled.reshape(row_count, width), w_in, preferred_element_type=jnp.float32) + b_in
    )
    out_grad = (
        (layer_scale * cot_full.astype(jnp.float32)).astype(jnp.bfloat16).reshape(row_count, width)
    )
    hidden_grad = lax.dot_general(
        out_grad, w_out, (((1,), (1,)), ((), ())), preferred_element_type=jnp.float32
    )
    act_grad = (hidden_grad * gelu_slope(pre_act)).astype(jnp.bfloat16)
    partial_norm = lax.dot_general(
        act_grad, w_in, (((1,), (1,)), ((), ())), preferred_element_type=jnp.float32
    )
    first_channel = my_part * share
    norm_grad = lax.psum(partial_norm, "ch").reshape(most, TS, TS, width)
    weighted = norm_grad * ln_gain
    upstream_full = inv_std * (
        weighted
        - jnp.mean(weighted, axis=3, keepdims=True)
        - normed * jnp.mean(weighted * normed, axis=3, keepdims=True)
    )
    upstream = lax.dynamic_slice_in_dim(upstream_full, first_channel, share, 3)
    listed_mask = (slots < my_count).astype(jnp.float32)
    tile_grad = depthwise_back(upstream, dw_kernel)
    tile_grad = tile_grad.at[:, 3 : 3 + TS, 3 : 3 + TS, :].add(cot_mine.astype(jnp.float32))
    send_back = (
        jnp.zeros((buffer_len, framed_side, framed_side, share), jnp.float32)
        .at[pick]
        .set(tile_grad)
    )
    returned = lax.all_to_all(send_back, "img", split_axis=0, concat_axis=0, tiled=True)
    own_grads = returned[position] * listed_mask[:, None, None, None]
    span = jnp.arange(framed_side, dtype=jnp.int32)
    row_index = tile_offsets[:, 0][:, None, None] + span[None, :, None]
    col_index = tile_offsets[:, 1][:, None, None] + span[None, None, :]
    total = (
        jnp.zeros((side + 6, side + 6, share), jnp.float32).at[row_index, col_index].add(own_grads)
    )
    cropped = total[3 : 3 + side, 3 : 3 + side, :]
    return jnp.where(inside[:, :, None], cropped, jnp.zeros_like(cropped))


def solution(mesh):
    return jax.shard_map(
        shards,
        mesh=mesh,
        in_specs=(
            P("img", None, "ch"),
            P("img", None),
            P(),
            P("img", None),
            P("img", None, None, "ch"),
            P(None, "ch"),
            P("ch"),
            P(),
            P(),
            P(None, "ch"),
            P("ch"),
            P("ch", None),
            P(),
        ),
        out_specs=P("img", None, "ch"),
        check_vma=False,
    )
```

profile of v0, /device:TPU:0, one launch (start us, length us, event | category | flops | bytes accessed | tf_op | source)
XLA Modules:
  0.0 1014.0 jit_solution(13687951348938377667)
XLA Ops:
  27.0 81.8 %while.51 = (s32[]{:T(128)}, bf16[38,38,384]{2,1,0:T(8,128)(2,1)S(1)}, s32[32,3]{0,1:T(4,128)S(1)}, bf16[32,10,10,384]{3,2,1,0:T(8,128)(2,1)}, s32[]{:T(128)}) while((s32[]{:T(128)}, bf16[38,38,384]{2,1,0:T(8,128)(2,1)S(1)}, s32[32,3]{0,1:T(4,128)S(1)}, bf16[32,10,10,384]{3,2,1,0:T(8,128)(2,1)}, s32[]{:T(128)}) %tuple.286), condition=%wide.while_cond.50, body=%wide.while_body.50.sunk | while | flops 2 | bytes 201321 | solution.py:70
  111.1 11.1 %scatter_fusion = bf16[32,10,10,384]{3,2,1,0:T(8,128)(2,1)} fusion(bf16[32,10,10,384]{3,2,1,0:T(8,128)(2,1)} %broadcast_in_dim.34, s32[32]{0:T(128)S(1)} %fusion.33, bf16[32,10,10,384]{3,2,1,0:T(8,128)(2,1)} %get-tuple-element.612), kind=kCustom, calls=%fused_computation.3 | custom fusion | bytes 7372928 | tf_op jit(solution)/shard_map/scatter | solution.py:91
  131.9 48.5 %all-to-all-done = bf16[32,10,10,384]{3,2,1,0:T(8,128)(2,1)} async-done(((bf16[32,10,10,384]{3,2,1,0:T(8,128)(2,1)}), bf16[32,10,10,384]{3,2,1,0:T(8,128)(2,1)}, u32[]{:S(2)}, u32[]{:S(2)}) %all-to-all-start) | async-done | bytes 2457632 | tf_op jit(solution)/shard_map/all_to_all | solution.py:94
  185.6 30.9 %add_convert_fusion.1 = bf16[32,4,4,384]{3,2,1,0:T(4,128)(2,1)} fusion(bf16[32,10,10,384]{3,2,1,0:T(8,128)(2,1)} %gather_fusion, f32[384]{0:T(512)S(1)} %get-tuple-element.660, f32[384]{0:T(512)S(1)} %get-tuple-element.661, f32[384]{0:T(512)S(1)} %get-tuple-element.614, f32[384]{0:T(512)S(1)} %get-tuple-element.615, f32[384]{0:T(512)S(1)} %get-tuple-element.616, ...), kind=kLoop, calls=%fused_computation.99 | loop fusion | flops 29097984 | bytes 19737600 | tf_op jit(solution)/shard_map/convert_element_type | solution.py:97
  219.4 25.5 %all-gather.4.cloned.1.call-done = bf16[32,4,4,1536]{3,2,1,0:T(4,128)(2,1)} async-done(((bf16[32,4,4,384]{3,2,1,0:T(4,128)(2,1)}), bf16[32,4,4,1536]{3,2,1,0:T(4,128)(2,1)}) %all-gather.4.cloned.1.call-update) | async-done | bytes 1572880 | tf_op jit(solution)/shard_map/all_gather | solution.py:100
  261.9 11.7 %fusion.26 = f32[512,1536]{1,0:T(8,128)} fusion(bf16[1536,1536]{1,0:T(8,128)(2,1)} %param.122, f32[512,1536]{1,0:T(8,128)} %convolution_add_fusion, bf16[512,1536]{1,0:T(8,128)(2,1)S(1)} %reshape.2695, bf16[1536,1536]{1,0:T(8,128)(2,1)} %param.124), kind=kOutput, calls=%fused_computation.101 | convolution fusion | flops 4846780416 | bytes 17301504 | tf_op jit(solution)/shard_map/dot_general | solution.py:120
  278.9 71.7 %all-reduce.4.cloned.1.call-done = f32[512,1536]{1,0:T(8,128)} async-done(((f32[512,1536]{1,0:T(8,128)}), f32[512,1536]{1,0:T(8,128)}) %all-reduce.4.cloned.1.call-update) | async-done | bytes 3145744 | tf_op jit(solution)/shard_map/psum | solution.py:124
  368.0 10.8 %scatter-add.175 = f32[32,10,10,384]{3,2,1,0:T(8,128)} dynamic-update-slice(f32[32,10,10,384]{3,2,1,0:T(8,128)} %scatter-add.174, f32[32,4,4,384]{3,2,1,0:T(4,128)S(1)} %fusion.11, s32[]{:T(128)} %constant.1568.clone.1, s32[]{:T(128)} %bitcast.6, s32[]{:T(128)} %bitcast.7, s32[]{:T(128)} %constant.1568.clone.1) | dynamic-update-slice | bytes 1572868 | tf_op jit(solution)/shard_map/scatter-add | solution.py:34
  382.9 10.7 %scatter-add.176 = f32[32,10,10,384]{3,2,1,0:T(8,128)} dynamic-update-slice(f32[32,10,10,384]{3,2,1,0:T(8,128)} %scatter-add.175, f32[32,4,4,384]{3,2,1,0:T(4,128)S(1)} %add_select_fusion.4, s32[]{:T(128)} %constant.1568.clone.1, s32[]{:T(128)} %bitcast.8, s32[]{:T(128)} %bitcast.9, s32[]{:T(128)} %constant.1568.clone.1) | dynamic-update-slice | bytes 1572868 | tf_op jit(solution)/shard_map/scatter-add | solution.py:34
  397.5 10.5 %scatter-add.179 = f32[32,10,10,384]{3,2,1,0:T(8,128)} dynamic-update-slice(f32[32,10,10,384]{3,2,1,0:T(8,128)} %scatter-add.176, f32[32,4,4,384]{3,2,1,0:T(4,128)S(1)} %add_select_fusion.3, s32[]{:T(128)} %constant.1568.clone.1, s32[]{:T(128)} %bitcast.10, s32[]{:T(128)} %bitcast.11, s32[]{:T(128)} %constant.1568.clone.1) | dynamic-update-slice | bytes 1572868 | tf_op jit(solution)/shard_map/scatter-add | solution.py:34
  412.0 10.7 %scatter-add.180 = f32[32,10,10,384]{3,2,1,0:T(8,128)} dynamic-update-slice(f32[32,10,10,384]{3,2,1,0:T(8,128)} %scatter-add.179, f32[32,4,4,384]{3,2,1,0:T(4,128)S(1)} %add_select_fusion.2, s32[]{:T(128)} %constant.1568.clone.1, s32[]{:T(128)} %bitcast.12, s32[]{:T(128)} %bitcast.13, s32[]{:T(128)} %constant.1568.clone.1) | dynamic-update-slice | bytes 1572868 | tf_op jit(solution)/shard_map/scatter-add | solution.py:34
  426.8 10.7 %scatter-add.181 = f32[32,10,10,384]{3,2,1,0:T(8,128)} dynamic-update-slice(f32[32,10,10,384]{3,2,1,0:T(8,128)} %scatter-add.180, f32[32,4,4,384]{3,2,1,0:T(4,128)S(1)} %add_select_fusion.1, s32[]{:T(128)} %constant.1568.clone.1, s32[]{:T(128)} %bitcast.14, s32[]{:T(128)} %bitcast.15, s32[]{:T(128)} %constant.1568.clone.1) | dynamic-update-slice | bytes 1572868 | tf_op jit(solution)/shard_map/scatter-add | solution.py:34
  441.6 10.6 %scatter-add.184 = f32[32,10,10,384]{3,2,1,0:T(8,128)} dynamic-update-slice(f32[32,10,10,384]{3,2,1,0:T(8,128)} %scatter-add.181, f32[32,4,4,384]{3,2,1,0:T(4,128)S(1)} %add_select_fusion, s32[]{:T(128)} %constant.1568.clone.1, s32[]{:T(128)} %bitcast.16, s32[]{:T(128)} %bitcast.17, s32[]{:T(128)} %constant.1568.clone.1) | dynamic-update-slice | bytes 1572868 | tf_op jit(solution)/shard_map/scatter-add | solution.py:34
  518.0 9.4 scatter-add.199
  579.4 9.8 scatter-add.210
  590.9 9.4 scatter-add.211
  601.9 9.4 scatter-add.214
  616.1 9.4 scatter-add.216
  627.7 9.4 scatter-add.219
  775.1 9.5 scatter-add.246
  823.0 9.4 scatter-add.306
  836.5 15.6 %scatter_fusion.2 = f32[32,10,10,384]{3,2,1,0:T(8,128)} fusion(f32[32,10,10,384]{3,2,1,0:T(8,128)} %broadcast.1148, s32[32]{0:T(128)S(1)} %fusion.32, f32[32,10,10,384]{3,2,1,0:T(8,128)} %scatter-add.306), kind=kCustom, calls=%fused_computation.5 | custom fusion | bytes 14745728 | tf_op jit(solution)/shard_map/scatter | solution.py:138
  861.6 96.7 %all-to-all-done.2 = f32[32,10,10,384]{3,2,1,0:T(8,128)} async-done(((f32[32,10,10,384]{3,2,1,0:T(8,128)}), f32[32,10,10,384]{3,2,1,0:T(8,128)}, u32[]{:S(2)}, u32[]{:S(2)}) %all-to-all-start.2) | async-done | bytes 4915232 | tf_op jit(solution)/shard_map/all_to_all | solution.py:140
  979.9 22.7 %scatter_custom_fusion.3 = f32[1444,384]{1,0:T(8,128)S(1)} fusion(s32[3200]{0:T(1024)S(1)} %reshape.2834, f32[3200,384]{1,0:T(8,128)} %reshape.2836, f32[]{:T(128)} %constant.1567.clone.1), kind=kCustom, calls=%fused_computation.37 | custom fusion | flops 1228800 | bytes 2218496
  (269 shorter events, 526.3 us)
Async XLA Ops:
  12.2 110.0 %all-to-all-start.1 = ((bf16[32,4,4,384]{3,2,1,0:T(4,128)(2,1)}), bf16[32,4,4,384]{3,2,1,0:T(4,128)(2,1)S(1)}, u32[]{:S(2)}, u32[]{:S(2)}) async-start(bf16[32,4,4,384]{3,2,1,0:T(4,128)(2,1)} %scatter_fusion.1), calls=%async_computation.1 | async-start | bytes 786432 | tf_op jit(solution)/shard_map/all_to_all | solution.py:95
  122.2 7.7 copy-start.3
  122.2 58.2 %all-to-all-start = ((bf16[32,10,10,384]{3,2,1,0:T(8,128)(2,1)}), bf16[32,10,10,384]{3,2,1,0:T(8,128)(2,1)}, u32[]{:S(2)}, u32[]{:S(2)}) async-start(bf16[32,10,10,384]{3,2,1,0:T(8,128)(2,1)} %scatter_fusion), calls=%async_computation | async-start | bytes 7864320 | tf_op jit(solution)/shard_map/all_to_all | solution.py:94
  129.8 55.7 %copy-start.8 = (f32[384]{0:T(512)S(1)}, f32[384]{0:T(512)}, u32[]{:S(2)}) copy-start(f32[384]{0:T(512)} %param.119) | copy-start | bytes 4612
  129.9 86.7 %all-gather.6.cloned.1.call-start = ((), (), s32[]{:S(2)}) async-start(), calls=%async_computation.5 | async-start | bytes 1966080 | tf_op jit(solution)/shard_map/all_gather | solution.py:101
  131.9 113.0 %all-gather.4.cloned.1.call-start = ((), (), s32[]{:S(2)}) async-start(), calls=%async_computation.3 | async-start | bytes 1966080 | tf_op jit(solution)/shard_map/all_gather | solution.py:100
  185.6 31.0 %copy-start.5 = (f32[1536]{0:T(1024)S(1)}, f32[1536]{0:T(1024)}, u32[]{:S(2)}) copy-start(f32[1536]{0:T(1024)} %param.125) | copy-start | bytes 18436
  216.5 33.2 %copy-start.4 = (f32[1536]{0:T(1024)S(1)}, f32[1536]{0:T(1024)}, u32[]{:S(2)}) copy-start(f32[1536]{0:T(1024)} %param.120) | copy-start | bytes 18436
  216.5 33.2 %copy-start.6 = (f32[1536]{0:T(1024)S(1)}, f32[1536]{0:T(1024)}, u32[]{:S(2)}) copy-start(f32[1536]{0:T(1024)} %param.121) | copy-start | bytes 18436
  216.5 134.1 %all-reduce.4.cloned.1.call-start = ((), (), s32[]{:S(2)}) async-start(), calls=%async_computation.4 | async-start | bytes 6291456 | tf_op jit(solution)/shard_map/psum | solution.py:124
  249.7 5.1 copy-start.10
  261.9 15.5 %copy-start.7 = (s32[4]{0:T(128)S(1)}, s32[4]{0:T(128)}, u32[]{:S(2)}) copy-start(s32[4]{0:T(128)} %constant.1590.clone.1) | copy-start | bytes 52
  273.6 81.9 %copy-start = (bf16[32,4,4,1536]{3,2,1,0:T(4,128)(2,1)S(1)}, bf16[32,4,4,1536]{3,2,1,0:T(4,128)(2,1)}, u32[]{:S(2)}) copy-start(bf16[32,4,4,1536]{3,2,1,0:T(4,128)(2,1)} %all-gather.4.cloned.1.call-done) | copy-start | bytes 4718596
  355.5 4.6 copy-start.1
  795.6 25.7 %copy-start.2 = (bf16[32,4,4,384]{3,2,1,0:T(4,128)(2,1)S(1)}, bf16[32,4,4,384]{3,2,1,0:T(4,128)(2,1)}, u32[]{:S(2)}) copy-start(bf16[32,4,4,384]{3,2,1,0:T(4,128)(2,1)} %gather_fusion.1) | copy-start | bytes 1179652
  852.0 7.7 copy-start.9
  852.0 8.3 copy-start.11
  852.0 106.3 %all-to-all-start.2 = ((f32[32,10,10,384]{3,2,1,0:T(8,128)}), f32[32,10,10,384]{3,2,1,0:T(8,128)}, u32[]{:S(2)}, u32[]{:S(2)}) async-start(f32[32,10,10,384]{3,2,1,0:T(8,128)} %scatter_fusion.2), calls=%async_computation.2 | async-start | bytes 15728640 | tf_op jit(solution)/shard_map/all_to_all | solution.py:140
Sparse Core Ops, SparseCore 0:
  132.3 32.7 all-gather.5
  216.6 28.2 all-gather.3
  273.7 76.8 all-reduce.3
where the time goes:
time: 1030 us; the launch traced here: 1010 us
  local copies, waits for them, and re-layouts  516 us (50%)
  waiting for transfers between devices  242 us (23%)
  other arithmetic  200 us (19%)
  starting transfers between devices  22.4 us (2%)
  matrix products  18.8 us (2%)
  between operations  13.8 us (1%)
    scatter-add x37, local copies, waits for them, and re-layouts, depthwise_back(): result.at[:, offset_r:offset_r + TS, offset_c:offset_c + TS, :]  349 us
    all_to_all x1, waiting for transfers between devices, shards(): lax.all_to_all(send_back, 'img', split_axis=0, concat_axis=0, tiled=True)  96.7 us
    gather x96, local copies, waits for them, and re-layouts  81.8 us
    psum x1, waiting for transfers between devices, shards(): norm_grad = lax.psum(partial_norm, 'ch').reshape(most, TS, TS, width)  71.7 us
    add x31, other arithmetic, depthwise_back(): result.at[:, offset_r:offset_r + TS, offset_c:offset_c + TS, :]  57.6 us
    all_to_all x1, waiting for transfers between devices, shards(): lax.all_to_all(send_tiles, 'img', split_axis=0, concat_axis=0, tiled=True)  48.5 us
    scatter-add x12, other arithmetic, depthwise_back(): result.at[:, offset_r:offset_r + TS, offset_c:offset_c + TS, :]  32.1 us
    convert_element_type x1, other arithmetic, shards(): mixed = depthwise(got_tiles[pick], dw_kernel, dw_bias).astype(jnp.bfloat16)  30.9 us
  transfers between devices with their start and end apart: 6, of which 4 were waited for; matrix products, arithmetic and copies ran while one was open for 15% of the time, Pallas kernels for 0%

commit v1 on v0

--- a/solution.py
+++ b/solution.py
@@ -1,3 +1,4 @@
+import functools
 import jax
 import jax.numpy as jnp
 from jax import lax
@@ -7,6 +8,33 @@
 slope_coef = 0.7978845608
 cubic_coef = 0.044715
 norm_eps = 1e-06
+
+
+def trace_the_cubes(m, dim_at):
+    m = jnp.moveaxis(m, 0, dim_at)
+    q_next = m.shape
+    return m.reshape(*q_next[:dim_at], q_next[dim_at] * q_next[dim_at + 1], *q_next[dim_at + 2 :])
+
+
+def draw_the_packet(my_data, group_axis, dim_i):
+    n = lax.axis_size(group_axis)
+    ledger = [(src_i, (src_i + 1) % n) for src_i in range(n)]
+    lanes = [(b, p) for p, b in ledger]
+    w_next, current_value = ([], [])
+    for d in [*range(n - 1)]:
+        if d % 2 == 0:
+            w_next.append(lax.ppermute(w_next[-1] if w_next else my_data, group_axis, ledger))
+        else:
+            current_value.append(
+                lax.ppermute(current_value[-1] if current_value else my_data, group_axis, lanes)
+            )
+    local_now = jnp.stack([*w_next[::-1], my_data, *current_value])
+    last = lax.axis_index(group_axis) - len(w_next)
+    local_now = local_now[(jnp.arange(n) - last) % n]
+    return trace_the_cubes(local_now, dim_i)
+
+
+_update_notes = functools.partial(draw_the_packet, group_axis="ch", dim_i=3)
 
 
 def gelu_slope(pre_act):
@@ -96,10 +124,7 @@
     )
     mixed = depthwise(got_tiles[pick], dw_kernel, dw_bias).astype(jnp.bfloat16)
     cot_mine = got_cot[pick]
-    gathered, cot_full = (
-        lax.all_gather(mixed, "ch", axis=3, tiled=True),
-        lax.all_gather(cot_mine, "ch", axis=3, tiled=True),
-    )
+    gathered, cot_full = (_update_notes(mixed), lax.all_gather(cot_mine, "ch", axis=3, tiled=True))
     values = gathered.astype(jnp.float32)
     center = jnp.mean(values, axis=3, keepdims=True)
     spread = jnp.mean(jnp.square(values - center), axis=3, keepdims=True)

time: 1030 us -> 1030 us (level)
  waiting for transfers between devices: 242 us -> 214 us
  other arithmetic: 200 us -> 213 us
    all_gather x1 -> x0, waiting for transfers between devices: 25.5 us -> none  [shards(): lax.all_gather(mixed, 'ch', axis=3, tiled=True)]
    another operation x10 -> x12, other arithmetic: 21.7 us -> 36.4 us
    unnamed x4 -> x5, other arithmetic: 23.2 us -> 26.7 us
    gather x96 -> x97, local copies, waits for them, and re-layouts: 81.8 us -> 84 us
  transfers between devices with their start and end apart: 6 -> 8, of which waited for: 4 -> 4; matrix products, arithmetic and copies ran while one was open for 15% -> 17% of each run, Pallas kernels for 0% -> 0%
where the time goes in v1:
time: 1030 us; the launch traced here: 1010 us
  local copies, waits for them, and re-layouts  525 us (51%)
  waiting for transfers between devices  214 us (21%)
  other arithmetic  213 us (21%)
  starting transfers between devices  27.3 us (3%)
  matrix products  18.6 us (2%)
  between operations  14.8 us (1%)
    scatter-add x37, local copies, waits for them, and re-layouts, depthwise_back(): result.at[:, offset_r:offset_r + TS, offset_c:offset_c + TS, :]  348 us
    all_to_all x1, waiting for transfers between devices, shards(): lax.all_to_all(send_back, 'img', split_axis=0, concat_axis=0, tiled=True)  96.7 us
    gather x96, local copies, waits for them, and re-layouts  81.8 us
    psum x1, waiting for transfers between devices, shards(): norm_grad = lax.psum(partial_norm, 'ch').reshape(most, TS, TS, width)  65.2 us
    add x31, other arithmetic, depthwise_back(): result.at[:, offset_r:offset_r + TS, offset_c:offset_c + TS, :]  57.7 us
    all_to_all x1, waiting for transfers between devices, shards(): lax.all_to_all(send_tiles, 'img', split_axis=0, concat_axis=0, tiled=True)  46.5 us
    scatter-add x12, other arithmetic, depthwise_back(): result.at[:, offset_r:offset_r + TS, offset_c:offset_c + TS, :]  32.1 us
    convert_element_type x1, other arithmetic, shards(): mixed = depthwise(got_tiles[pick], dw_kernel, dw_bias).astype(jnp.bfloat16)  30.5 us
  transfers between devices with their start and end apart: 8, of which 4 were waited for; matrix products, arithmetic and copies ran while one was open for 17% of the time, Pallas kernels for 0%

profile of v1, /device:TPU:0, one launch (start us, length us, event | category | flops | bytes accessed | tf_op | source)
XLA Modules:
  0.0 1011.8 jit_solution(11688979724497160857)
XLA Ops:
  27.6 81.8 %while.51 = (s32[]{:T(128)}, bf16[38,38,384]{2,1,0:T(8,128)(2,1)S(1)}, s32[32,3]{0,1:T(4,128)S(1)}, bf16[32,10,10,384]{3,2,1,0:T(8,128)(2,1)}, s32[]{:T(128)}) while((s32[]{:T(128)}, bf16[38,38,384]{2,1,0:T(8,128)(2,1)S(1)}, s32[32,3]{0,1:T(4,128)S(1)}, bf16[32,10,10,384]{3,2,1,0:T(8,128)(2,1)}, s32[]{:T(128)}) %tuple.286), condition=%wide.while_cond.50, body=%wide.while_body.50.sunk | while | flops 2 | bytes 201321 | solution.py:98
  111.6 11.1 %scatter_fusion = bf16[32,10,10,384]{3,2,1,0:T(8,128)(2,1)} fusion(bf16[32,10,10,384]{3,2,1,0:T(8,128)(2,1)} %broadcast_in_dim.34, s32[32]{0:T(128)S(1)} %fusion.39, bf16[32,10,10,384]{3,2,1,0:T(8,128)(2,1)} %get-tuple-element.612), kind=kCustom, calls=%fused_computation.4 | custom fusion | bytes 7372928 | tf_op jit(solution)/shard_map/scatter | solution.py:119
  134.6 46.5 %all-to-all-done = bf16[32,10,10,384]{3,2,1,0:T(8,128)(2,1)} async-done(((bf16[32,10,10,384]{3,2,1,0:T(8,128)(2,1)}), bf16[32,10,10,384]{3,2,1,0:T(8,128)(2,1)}, u32[]{:S(2)}, u32[]{:S(2)}) %all-to-all-start) | async-done | bytes 2457632 | tf_op jit(solution)/shard_map/all_to_all | solution.py:122
  186.2 30.5 %add_convert_fusion.2 = bf16[32,4,4,384]{3,2,1,0:T(4,128)(2,1)S(1)} fusion(bf16[32,10,10,384]{3,2,1,0:T(8,128)(2,1)} %gather_fusion, f32[384]{0:T(512)S(1)} %get-tuple-element.662, f32[384]{0:T(512)S(1)} %get-tuple-element.663, f32[384]{0:T(512)S(1)} %get-tuple-element.616, f32[384]{0:T(512)S(1)} %get-tuple-element.617, f32[384]{0:T(512)S(1)} %get-tuple-element.618, ...), kind=kLoop, calls=%fused_computation.107 | loop fusion | flops 29097984 | bytes 19737600 | tf_op jit(solution)/shard_map/convert_element_type | solution.py:125
  221.7 12.2 %fusion.59 = bf16[1,32,4,4,384]{4,3,2,1,0:T(4,128)(2,1)S(1)} fusion(f32[384]{0:T(512)S(1)} %get-tuple-element.662, bf16[32,10,10,384]{3,2,1,0:T(8,128)(2,1)S(1)} %copy-done, f32[384]{0:T(512)S(1)} %get-tuple-element.663, f32[384]{0:T(512)S(1)} %get-tuple-element.616, f32[384]{0:T(512)S(1)} %get-tuple-element.617, f32[384]{0:T(512)S(1)} %get-tuple-element.618, ...), kind=kLoop, calls=%fused_computation.248 | loop fusion | flops 29097984 | bytes 19737600 | tf_op jit(solution)/shard_map/stack | solution.py:31
  267.1 11.8 %fusion.31 = f32[512,1536]{1,0:T(8,128)} fusion(bf16[1536,1536]{1,0:T(8,128)(2,1)} %param.122, f32[512,1536]{1,0:T(8,128)} %convolution_add_fusion, bf16[512,1536]{1,0:T(8,128)(2,1)S(1)} %copy-done.5, bf16[1536,1536]{1,0:T(8,128)(2,1)} %param.124), kind=kOutput, calls=%fused_computation.109 | convolution fusion | flops 4846780416 | bytes 17301504 | tf_op jit(solution)/shard_map/dot_general | solution.py:145
  286.9 65.2 %all-reduce.4.cloned.1.call-done = f32[512,1536]{1,0:T(8,128)} async-done(((f32[512,1536]{1,0:T(8,128)}), f32[512,1536]{1,0:T(8,128)}) %all-reduce.4.cloned.1.call-update) | async-done | bytes 3145744 | tf_op jit(solution)/shard_map/psum | solution.py:149
  365.9 10.7 %scatter-add.175 = f32[32,10,10,384]{3,2,1,0:T(8,128)} dynamic-update-slice(f32[32,10,10,384]{3,2,1,0:T(8,128)} %scatter-add.174, f32[32,4,4,384]{3,2,1,0:T(4,128)S(1)} %fusion.13, s32[]{:T(128)} %constant.1584.clone.1, s32[]{:T(128)} %bitcast.12, s32[]{:T(128)} %bitcast.13, s32[]{:T(128)} %constant.1584.clone.1) | dynamic-update-slice | bytes 1572868 | tf_op jit(solution)/shard_map/scatter-add | solution.py:62
  380.6 10.5 %scatter-add.176 = f32[32,10,10,384]{3,2,1,0:T(8,128)} dynamic-update-slice(f32[32,10,10,384]{3,2,1,0:T(8,128)} %scatter-add.175, f32[32,4,4,384]{3,2,1,0:T(4,128)S(1)} %add_select_fusion.4, s32[]{:T(128)} %constant.1584.clone.1, s32[]{:T(128)} %bitcast.14, s32[]{:T(128)} %bitcast.15, s32[]{:T(128)} %constant.1584.clone.1) | dynamic-update-slice | bytes 1572868 | tf_op jit(solution)/shard_map/scatter-add | solution.py:62
  395.1 10.6 %scatter-add.179 = f32[32,10,10,384]{3,2,1,0:T(8,128)} dynamic-update-slice(f32[32,10,10,384]{3,2,1,0:T(8,128)} %scatter-add.176, f32[32,4,4,384]{3,2,1,0:T(4,128)S(1)} %add_select_fusion.3, s32[]{:T(128)} %constant.1584.clone.1, s32[]{:T(128)} %bitcast.16, s32[]{:T(128)} %bitcast.17, s32[]{:T(128)} %constant.1584.clone.1) | dynamic-update-slice | bytes 1572868 | tf_op jit(solution)/shard_map/scatter-add | solution.py:62
  409.7 10.5 %scatter-add.180 = f32[32,10,10,384]{3,2,1,0:T(8,128)} dynamic-update-slice(f32[32,10,10,384]{3,2,1,0:T(8,128)} %scatter-add.179, f32[32,4,4,384]{3,2,1,0:T(4,128)S(1)} %add_select_fusion.2, s32[]{:T(128)} %constant.1584.clone.1, s32[]{:T(128)} %bitcast.18, s32[]{:T(128)} %bitcast.19, s32[]{:T(128)} %constant.1584.clone.1) | dynamic-update-slice | bytes 1572868 | tf_op jit(solution)/shard_map/scatter-add | solution.py:62
  424.3 10.6 %scatter-add.181 = f32[32,10,10,384]{3,2,1,0:T(8,128)} dynamic-update-slice(f32[32,10,10,384]{3,2,1,0:T(8,128)} %scatter-add.180, f32[32,4,4,384]{3,2,1,0:T(4,128)S(1)} %add_select_fusion.1, s32[]{:T(128)} %constant.1584.clone.1, s32[]{:T(128)} %bitcast.20, s32[]{:T(128)} %bitcast.21, s32[]{:T(128)} %constant.1584.clone.1) | dynamic-update-slice | bytes 1572868 | tf_op jit(solution)/shard_map/scatter-add | solution.py:62
  438.9 10.5 %scatter-add.184 = f32[32,10,10,384]{3,2,1,0:T(8,128)} dynamic-update-slice(f32[32,10,10,384]{3,2,1,0:T(8,128)} %scatter-add.181, f32[32,4,4,384]{3,2,1,0:T(4,128)S(1)} %add_select_fusion, s32[]{:T(128)} %constant.1584.clone.1, s32[]{:T(128)} %bitcast.22, s32[]{:T(128)} %bitcast.23, s32[]{:T(128)} %constant.1584.clone.1) | dynamic-update-slice | bytes 1572868 | tf_op jit(solution)/shard_map/scatter-add | solution.py:62
  515.2 9.4 scatter-add.199
  576.8 9.4 scatter-add.210
  587.8 9.4 scatter-add.211
  598.9 9.4 scatter-add.214
  613.1 9.4 scatter-add.216
  624.6 9.4 scatter-add.219
  699.8 9.7 scatter-add.234
  820.4 9.4 scatter-add.306
  833.8 15.6 %scatter_fusion.2 = f32[32,10,10,384]{3,2,1,0:T(8,128)} fusion(f32[32,10,10,384]{3,2,1,0:T(8,128)} %broadcast.1228, s32[32]{0:T(128)S(1)} %copy-done.93, f32[32,10,10,384]{3,2,1,0:T(8,128)} %scatter-add.306), kind=kCustom, calls=%fused_computation.6 | custom fusion | bytes 14745728 | tf_op jit(solution)/shard_map/scatter | solution.py:163
  859.2 96.7 %all-to-all-done.2 = f32[32,10,10,384]{3,2,1,0:T(8,128)} async-done(((f32[32,10,10,384]{3,2,1,0:T(8,128)}), f32[32,10,10,384]{3,2,1,0:T(8,128)}, u32[]{:S(2)}, u32[]{:S(2)}) %all-to-all-start.2) | async-done | bytes 4915232 | tf_op jit(solution)/shard_map/all_to_all | solution.py:165
  977.5 22.7 %scatter_custom_fusion.3 = f32[1444,384]{1,0:T(8,128)S(1)} fusion(s32[3200]{0:T(1024)S(1)} %reshape.2920, f32[3200,384]{1,0:T(8,128)} %reshape.2922, f32[]{:T(128)} %constant.1583.clone.1), kind=kCustom, calls=%fused_computation.42 | custom fusion | flops 1228800 | bytes 2218496
  (460 shorter events, 546.0 us)
Async XLA Ops:
  6.6 105.1 %copy-start.90 = (s32[32]{0:T(128)}, s32[32]{0:T(128)S(1)}, u32[]{:S(2)}) copy-start(s32[32]{0:T(128)S(1)} %fusion.39) | copy-start | bytes 388
  12.2 110.6 %all-to-all-start.1 = ((bf16[32,4,4,384]{3,2,1,0:T(4,128)(2,1)}), bf16[32,4,4,384]{3,2,1,0:T(4,128)(2,1)S(1)}, u32[]{:S(2)}, u32[]{:S(2)}) async-start(bf16[32,4,4,384]{3,2,1,0:T(4,128)(2,1)} %scatter_fusion.1), calls=%async_computation.1 | async-start | bytes 786432 | tf_op jit(solution)/shard_map/all_to_all | solution.py:123
  122.8 58.2 %all-to-all-start = ((bf16[32,10,10,384]{3,2,1,0:T(8,128)(2,1)}), bf16[32,10,10,384]{3,2,1,0:T(8,128)(2,1)}, u32[]{:S(2)}, u32[]{:S(2)}) async-start(bf16[32,10,10,384]{3,2,1,0:T(8,128)(2,1)} %scatter_fusion), calls=%async_computation | async-start | bytes 7864320 | tf_op jit(solution)/shard_map/all_to_all | solution.py:122
  130.4 103.6 %all-gather.3.cloned.1.call-start = ((), (), s32[]{:S(2)}) async-start(), calls=%async_computation.4 | async-start | bytes 1966080 | tf_op jit(solution)/shard_map/all_gather | solution.py:127
  131.8 89.5 %copy-start.80 = (f32[384]{0:T(512)}, f32[384]{0:T(512)S(1)}, u32[]{:S(2)}) copy-start(f32[384]{0:T(512)S(1)} %get-tuple-element.654) | copy-start | bytes 4612
  131.8 89.5 %copy-start.84 = (f32[384]{0:T(512)}, f32[384]{0:T(512)S(1)}, u32[]{:S(2)}) copy-start(f32[384]{0:T(512)S(1)} %get-tuple-element.655) | copy-start | bytes 4612
  131.8 89.5 %copy-start.86 = (f32[384]{0:T(512)}, f32[384]{0:T(512)S(1)}, u32[]{:S(2)}) copy-start(f32[384]{0:T(512)S(1)} %get-tuple-element.656) | copy-start | bytes 4612
  131.9 89.4 %copy-start.44 = (f32[384]{0:T(512)}, f32[384]{0:T(512)S(1)}, u32[]{:S(2)}) copy-start(f32[384]{0:T(512)S(1)} %get-tuple-element.635) | copy-start | bytes 4612
  131.9 89.4 %copy-start.48 = (f32[384]{0:T(512)}, f32[384]{0:T(512)S(1)}, u32[]{:S(2)}) copy-start(f32[384]{0:T(512)S(1)} %get-tuple-element.636) | copy-start | bytes 4612
  131.9 89.4 %copy-start.50 = (f32[384]{0:T(512)}, f32[384]{0:T(512)S(1)}, u32[]{:S(2)}) copy-start(f32[384]{0:T(512)S(1)} %get-tuple-element.637) | copy-start | bytes 4612
  131.9 89.4 %copy-start.52 = (f32[384]{0:T(512)}, f32[384]{0:T(512)S(1)}, u32[]{:S(2)}) copy-start(f32[384]{0:T(512)S(1)} %get-tuple-element.638) | copy-start | bytes 4612
  131.9 89.4 %copy-start.54 = (f32[384]{0:T(512)}, f32[384]{0:T(512)S(1)}, u32[]{:S(2)}) copy-start(f32[384]{0:T(512)S(1)} %get-tuple-element.639) | copy-start | bytes 4612
  132.0 89.4 %copy-start.56 = (f32[384]{0:T(512)}, f32[384]{0:T(512)S(1)}, u32[]{:S(2)}) copy-start(f32[384]{0:T(512)S(1)} %get-tuple-element.640) | copy-start | bytes 4612
  132.0 89.4 %copy-start.58 = (f32[384]{0:T(512)}, f32[384]{0:T(512)S(1)}, u32[]{:S(2)}) copy-start(f32[384]{0:T(512)S(1)} %get-tuple-element.641) | copy-start | bytes 4612
  132.0 89.4 %copy-start.60 = (f32[384]{0:T(512)}, f32[384]{0:T(512)S(1)}, u32[]{:S(2)}) copy-start(f32[384]{0:T(512)S(1)} %get-tuple-element.642) | copy-start | bytes 4612
  132.0 89.4 %copy-start.62 = (f32[384]{0:T(512)}, f32[384]{0:T(512)S(1)}, u32[]{:S(2)}) copy-start(f32[384]{0:T(512)S(1)} %get-tuple-element.643) | copy-start | bytes 4612
  132.0 89.4 %copy-start.64 = (f32[384]{0:T(512)}, f32[384]{0:T(512)S(1)}, u32[]{:S(2)}) copy-start(f32[384]{0:T(512)S(1)} %get-tuple-element.644) | copy-start | bytes 4612
  132.0 89.4 %copy-start.66 = (f32[384]{0:T(512)}, f32[384]{0:T(512)S(1)}, u32[]{:S(2)}) copy-start(f32[384]{0:T(512)S(1)} %get-tuple-element.645) | copy-start | bytes 4612
  132.0 89.4 %copy-start.68 = (f32[384]{0:T(512)}, f32[384]{0:T(512)S(1)}, u32[]{:S(2)}) copy-start(f32[384]{0:T(512)S(1)} %get-tuple-element.646) | copy-start | bytes 4612
  134.5 217.5 %all-reduce.4.cloned.1.call-start = ((), (), s32[]{:S(2)}) async-start(), calls=%async_computation.3 | async-start | bytes 6291456 | tf_op jit(solution)/shard_map/psum | solution.py:149
  216.7 17.2 %collective-permute-start = (bf16[32,4,4,384]{3,2,1,0:T(4,128)(2,1)S(1)}, bf16[32,4,4,384]{3,2,1,0:T(4,128)(2,1)S(1)}, u32[]{:S(2)}, u32[]{:S(2)}) collective-permute-start(bf16[32,4,4,384]{3,2,1,0:T(4,128)(2,1)S(1)} %add_convert_fusion.2), channel_id=1, source_target_pairs={{0,1},{1,2},{2,3},{3,0},{4,5},{5,6},{6,7},{7,4},{8,9},{9,10},{10,1... | collective-permute-start | bytes 1179656 | tf_op jit(solution)/shard_map/ppermute | solution.py:26
  218.7 19.0 %collective-permute-start.2 = (bf16[32,4,4,384]{3,2,1,0:T(4,128)(2,1)S(1)}, bf16[32,4,4,384]{3,2,1,0:T(4,128)(2,1)S(1)}, u32[]{:S(2)}, u32[]{:S(2)}) collective-permute-start(bf16[32,4,4,384]{3,2,1,0:T(4,128)(2,1)S(1)} %add_convert_fusion.2), channel_id=1, source_target_pairs={{1,0},{2,1},{3,2},{0,3},{5,4},{6,5},{7,6},{4,7},{9,8},{10,9},{11,1... | collective-permute-start | bytes 1179656 | tf_op jit(solution)/shard_map/ppermute | solution.py:29
  233.9 9.2 collective-permute-start.1
  849.4 106.5 %all-to-all-start.2 = ((f32[32,10,10,384]{3,2,1,0:T(8,128)}), f32[32,10,10,384]{3,2,1,0:T(8,128)}, u32[]{:S(2)}, u32[]{:S(2)}) async-start(f32[32,10,10,384]{3,2,1,0:T(8,128)} %scatter_fusion.2), calls=%async_computation.2 | async-start | bytes 15728640 | tf_op jit(solution)/shard_map/all_to_all | solution.py:165
  (85 other events, 3403.2 us)
Sparse Core Ops, SparseCore 0:
  134.6 32.7 all-gather.2
  279.0 73.0 all-reduce.3
